TPU v7x, 32 devices: a whole 2x2x4 slice. The times are simulated.
32 devices in a mesh: wide: 8 (over y, x, core), blk: 4 (over z).
Axes of the slice: x: 2, y: 2, z: 4, core: 2. Of those that a mesh axis runs over, the one named last changes fastest.
Arguments:
- tokens: bfloat16 [16384, 8192], P(('wide', 'blk')), may hold values from -6 to 6
- base_key_matrix: bfloat16 [8192, 1024], P('blk'), may hold values from -0.0625 to 0.0625
- adapter_down_weights: bfloat16 [256, 64, 8192], P(('wide', 'blk')), may hold values from -0.0625 to 0.0625
- adapter_up_weights: bfloat16 [256, 64, 1024], P(('wide', 'blk')), may hold values from -0.75 to 0.75
- request_adapter_index: int32 [256], P(('wide', 'blk')), may hold values from 0 to 255, as said below
Outputs:
- keys: bfloat16 [16384, 1024], P(('wide', 'blk'))
Inputs may be any that keep to these rules, and one draw needn't show every extreme that they name: `request_adapter_index`: request r lies on device r // 8 of wide+blk; adapter a lies on device a // 8. Each request's adapter lies on a device with the same blk index as the request. Of one device's requests at most 2 have adapters on any one wide index; for every blk index one wide index holds the adapters of exactly 2 requests of every device with that blk index.
All inputs are finite; a program needn't handle non-finite values.
Results may differ from a plain program's by a relative error of at most 0.005.
Values may be sent and summed in bfloat16 or wider, within the bound.
A program may use at most 192 MiB of HBM per device.

v0:
```python
import jax
import jax.numpy as jnp
from jax import lax
from jax.sharding import PartitionSpec as P

SEQ = 64
CAP = 2


def per_device(
    tokens, base_key_matrix, adapter_down_weights, adapter_up_weights, request_adapter_index
):
    wide_count = lax.axis_size("wide")
    block_count = lax.axis_size("blk")
    resident_count = adapter_down_weights.shape[0]
    req_count = request_adapter_index.shape[0]
    width = tokens.shape[1]
    out_width = base_key_matrix.shape[1]
    slot_count = wide_count * CAP
    base = jnp.dot(
        tokens,
        lax.all_gather(base_key_matrix, "blk", axis=0, tiled=True),
        preferred_element_type=jnp.float32,
    )
    owner_wide = request_adapter_index // (resident_count * block_count)
    local_ids = request_adapter_index % resident_count
    positions = jnp.arange(req_count, dtype=jnp.int32)
    same_owner = owner_wide[:, None] == owner_wide[None, :]
    earlier = positions[None, :] < positions[:, None]
    rank = jnp.sum(jnp.where(same_owner & earlier, 1, 0), axis=1).astype(jnp.int32)
    slot_of_req = owner_wide * CAP + rank
    member = slot_of_req[:, None] == jnp.arange(slot_count, dtype=jnp.int32)[None, :]
    valid = jnp.any(member, axis=0)
    source_req = jnp.sum(jnp.where(member, positions[:, None], 0), axis=0)
    slot_local = jnp.where(valid, jnp.take(local_ids, source_req, axis=0), 0)[:, None]
    requests = tokens.reshape(req_count, SEQ, width)
    outgoing = jnp.take(requests, source_req, axis=0)
    arrived, received_adapter_index = (
        lax.all_to_all(outgoing, "wide", split_axis=0, concat_axis=0, tiled=True),
        lax.all_to_all(slot_local, "wide", split_axis=0, concat_axis=0, tiled=True),
    )
    selected_down_weight = jnp.take(adapter_down_weights, received_adapter_index[:, 0], axis=0)
    selected_up_weight = jnp.take(adapter_up_weights, received_adapter_index[:, 0], axis=0)
    shrink = jnp.einsum(
        "sqd,srd->sqr", arrived, selected_down_weight, preferred_element_type=jnp.float32
    ).astype(jnp.bfloat16)
    expand = jnp.einsum(
        "sqr,srk->sqk", shrink, selected_up_weight, preferred_element_type=jnp.float32
    ).astype(jnp.bfloat16)
    returned = lax.all_to_all(expand, "wide", split_axis=0, concat_axis=0, tiled=True)
    delta = jnp.take(returned, slot_of_req, axis=0)
    keys = (base + delta.reshape(tokens.shape[0], out_width).astype(jnp.float32)).astype(
        jnp.bfloat16
    )
    return keys


def solution(mesh):
    return jax.shard_map(
        per_device,
        mesh=mesh,
        in_specs=(
            P(("wide", "blk"), None),
            P("blk", None),
            P(("wide", "blk"), None, None),
            P(("wide", "blk"), None, None),
            P(("wide", "blk")),
        ),
        out_specs=P(("wide", "blk"), None),
        check_vma=False,
    )
```

profile of v0, /device:TPU:1, one launch (start us, length us, event | category | flops | bytes accessed | tf_op | source)
XLA Modules:
  0.0 320.5 jit_solution(11483564231436792549)
XLA Ops:
  6.5 0.0 copy-start
  6.5 0.0 all-gather.2.cloned.1.call-start
  6.5 0.7 all-gather.2.cloned.1.call-update
  7.3 0.7 and_select_fusion
  7.9 0.2 select_reduce_fusion.1
  8.1 0.1 fusion.16
  8.2 0.1 reduce_or.12
  8.3 0.1 select_reduce_fusion
  8.4 0.1 reduce_sum.24
  8.5 0.7 gather_fusion
  9.1 0.1 gather.20
  9.2 0.6 select_select_fusion
  9.8 5.2 %all-to-all-start.1 = ((s32[8,2,1]{1,2,0:T(1,128)}), s32[8,2,1]{1,2,0:T(1,128)S(1)}, u32[]{:S(2)}, u32[]{:S(2)}) async-start(s32[8,2,1]{1,2,0:T(1,128)} %bitcast.3), calls=%async_computation.1 | async-start | bytes 8192 | tf_op jit(solution)/shard_map/all_to_all | solution.py:40
  15.1 12.4 %gather_fusion.3 = bf16[16,64,8192]{2,1,0:T(8,128)(2,1)} fusion(bf16[8,64,8192]{2,1,0:T(8,128)(2,1)} %bitcast.15, s32[1024]{0:T(1024)S(1)} %pad_clamp_fusion.4), kind=kCustom, calls=%fused_computation.clone | custom fusion | bytes 33554496 | tf_op jit(solution)/shard_map/jit(_take)/gather | solution.py:37
  27.5 14.5 %broadcast_select_fusion = bf16[16,64,8192]{2,1,0:T(8,128)(2,1)} fusion(bf16[16,64,8192]{2,1,0:T(8,128)(2,1)} %gather_fusion.3, pred[16]{0:T(512)(128)(4,1)S(1)} %compare_and_fusion.1), kind=kLoop, calls=%fused_computation.8 | loop fusion | flops 8388608 | bytes 33554448 | tf_op jit(solution)/shard_map/jit(_take)/select_n | solution.py:37
  42.0 0.0 all-to-all-done.1
  42.0 5.7 %all-to-all-start = ((bf16[16,64,8192]{2,1,0:T(8,128)(2,1)}), bf16[16,64,8192]{2,1,0:T(8,128)(2,1)}, u32[]{:S(2)}, u32[]{:S(2)}) async-start(bf16[16,64,8192]{2,1,0:T(8,128)(2,1)} %broadcast_select_fusion), calls=%async_computation | async-start | bytes 33554432 | tf_op jit(solution)/shard_map/all_to_all | solution.py:39
  47.6 0.1 all_to_all.14
  47.7 0.5 broadcast.225
  48.2 0.7 reduce.5
  48.9 0.1 squeeze.4
  49.0 0.0 copy-done
  49.0 0.7 gather_fusion.1
  49.7 10.5 %gather_fusion.4 = bf16[16,64,8192]{2,1,0:T(8,128)(2,1)} fusion(bf16[8,64,8192]{2,1,0:T(8,128)(2,1)} %param.9, s32[1024]{0:T(1024)S(1)} %pad_clamp_fusion.2), kind=kCustom, calls=%fused_computation.1.clone | custom fusion | bytes 33554496 | tf_op jit(solution)/shard_map/jit(_take)/gather | solution.py:42
  60.2 167.9 %all-to-all-done = bf16[16,64,8192]{2,1,0:T(8,128)(2,1)} async-done(((bf16[16,64,8192]{2,1,0:T(8,128)(2,1)}), bf16[16,64,8192]{2,1,0:T(8,128)(2,1)}, u32[]{:S(2)}, u32[]{:S(2)}) %all-to-all-start) | async-done | bytes 16777248 | tf_op jit(solution)/shard_map/all_to_all | solution.py:39
  228.1 14.6 %fusion.7 = bf16[16,64,1024]{2,1,0:T(8,128)(2,1)} fusion(bf16[16,64,1024]{2,1,0:T(8,128)(2,1)S(1)} %gather_fusion.1, pred[16]{0:T(512)(128)(4,1)S(1)} %compare_and_fusion, bf16[16,64,8192]{2,1,0:T(8,128)(2,1)} %all-to-all-done, bf16[16,64,8192]{2,1,0:T(8,128)(2,1)} %gather_fusion.4), kind=kOutput, calls=%fused_computation.14 | convolution fusion | flops 1218510848 | bytes 37748752 | tf_op jit(solution)/shard_map/sqr,srk->sqk/dot_general | solution.py:47
  242.7 7.1 %all-to-all-start.2 = ((bf16[16,64,1024]{2,1,0:T(8,128)(2,1)}), bf16[16,64,1024]{2,1,0:T(8,128)(2,1)S(1)}, u32[]{:S(2)}, u32[]{:S(2)}) async-start(bf16[16,64,1024]{2,1,0:T(8,128)(2,1)} %fusion.7), calls=%async_computation.2 | async-start | bytes 4194304 | tf_op jit(solution)/shard_map/all_to_all | solution.py:50
  249.7 0.1 broadcast_in_dim.69
  249.8 0.1 broadcast_in_dim.70
  249.9 23.0 %all-to-all-done.2 = bf16[16,64,1024]{2,1,0:T(8,128)(2,1)S(1)} async-done(((bf16[16,64,1024]{2,1,0:T(8,128)(2,1)}), bf16[16,64,1024]{2,1,0:T(8,128)(2,1)S(1)}, u32[]{:S(2)}, u32[]{:S(2)}) %all-to-all-start.2) | async-done | bytes 2097184 | tf_op jit(solution)/shard_map/all_to_all | solution.py:50
  272.9 1.6 gather_fusion.2
  274.4 1.4 bitcast_select_fusion
  275.8 22.2 %all-gather.2.cloned.1.call-done = bf16[8192,1024]{1,0:T(8,128)(2,1)} async-done(((bf16[2048,1024]{1,0:T(8,128)(2,1)}), bf16[8192,1024]{1,0:T(8,128)(2,1)}) %all-gather.2.cloned.1.call-update) | async-done | bytes 16777232 | tf_op jit(solution)/shard_map/all_gather | solution.py:22
  298.0 15.6 %add_convert_fusion = bf16[512,1024]{1,0:T(8,128)(2,1)} fusion(bf16[512,1024]{1,0:T(8,128)(2,1)S(1)} %bitcast_select_fusion, bf16[512,8192]{1,0:T(8,128)(2,1)} %param.7, bf16[8192,1024]{1,0:T(8,128)(2,1)} %all-gather.2.cloned.1.call-done), kind=kOutput, calls=%fused_computation.10 | convolution fusion | flops 8591507456 | bytes 27262976 | tf_op jit(solution)/shard_map/dot_general | solution.py:20
  (13 shorter events, 0.1 us)
Async XLA Ops:
  6.5 42.5 %copy-start = (bf16[8,64,1024]{2,1,0:T(8,128)(2,1)S(1)}, bf16[8,64,1024]{2,1,0:T(8,128)(2,1)}, u32[]{:S(2)}) copy-start(bf16[8,64,1024]{2,1,0:T(8,128)(2,1)} %param.10) | copy-start | bytes 3145732
  6.5 291.5 %all-gather.2.cloned.1.call-start = ((), (), s32[]{:S(2)}) async-start(), calls=%async_computation.3 | async-start | bytes 20971520 | tf_op jit(solution)/shard_map/all_gather | solution.py:22
  9.8 32.1 %all-to-all-start.1 = ((s32[8,2,1]{1,2,0:T(1,128)}), s32[8,2,1]{1,2,0:T(1,128)S(1)}, u32[]{:S(2)}, u32[]{:S(2)}) async-start(s32[8,2,1]{1,2,0:T(1,128)} %bitcast.3), calls=%async_computation.1 | async-start | bytes 8192 | tf_op jit(solution)/shard_map/all_to_all | solution.py:40
  42.0 186.1 %all-to-all-start = ((bf16[16,64,8192]{2,1,0:T(8,128)(2,1)}), bf16[16,64,8192]{2,1,0:T(8,128)(2,1)}, u32[]{:S(2)}, u32[]{:S(2)}) async-start(bf16[16,64,8192]{2,1,0:T(8,128)(2,1)} %broadcast_select_fusion), calls=%async_computation | async-start | bytes 33554432 | tf_op jit(solution)/shard_map/all_to_all | solution.py:39
  242.7 30.2 %all-to-all-start.2 = ((bf16[16,64,1024]{2,1,0:T(8,128)(2,1)}), bf16[16,64,1024]{2,1,0:T(8,128)(2,1)S(1)}, u32[]{:S(2)}, u32[]{:S(2)}) async-start(bf16[16,64,1024]{2,1,0:T(8,128)(2,1)} %fusion.7), calls=%async_computation.2 | async-start | bytes 4194304 | tf_op jit(solution)/shard_map/all_to_all | solution.py:50
Sparse Core Ops, SparseCore 0:
  8.9 289.0 all-gather.1
where the time goes:
time: 321 us; the launch traced here: 320 us
  waiting for transfers between devices  214 us (67%)
  matrix products  30.2 us (9%)
  local copies, waits for them, and re-layouts  26.9 us (8%)
  other arithmetic  18.2 us (6%)
  starting transfers between devices  17.9 us (6%)
  between operations  13.5 us (4%)
    all_to_all x1, waiting for transfers between devices, per_device(): lax.all_to_all(outgoing, 'wide', split_axis=0, concat_axis=0, tiled=True)  168 us
    all_to_all x1, waiting for transfers between devices, per_device(): lax.all_to_all(expand, 'wide', split_axis=0, concat_axis=0, tiled=True)  23 us
    all_gather x1, waiting for transfers between devices, per_device(): lax.all_gather(base_key_matrix, 'blk', axis=0, tiled=True)  22.2 us
    dot_general x1, matrix products, per_device(): jnp.dot(tokens, lax.all_gather(base_key_matrix, 'blk', axis=0, tiled=True...  15.6 us
    dot_general x1, matrix products, per_device(): jnp.einsum('sqr,srk->sqk', shrink, selected_up_weight, preferred_element_...  14.6 us
    select_n x2, other arithmetic, per_device(): outgoing = jnp.take(requests, source_req, axis=0)  14.5 us
    gather x1, local copies, waits for them, and re-layouts, per_device(): outgoing = jnp.take(requests, source_req, axis=0)  12.4 us
    gather x1, local copies, waits for them, and re-layouts, per_device(): jnp.take(adapter_down_weights, received_adapter_index[:, 0], axis=0)  10.5 us
  transfers between devices with their start and end apart: 4, of which 3 were waited for; matrix products, arithmetic and copies ran while one was open for 19% of the time, Pallas kernels for 0%

commit v1 on v0

v1 whole, which is shorter than its diff:
```python
import functools

import jax
import jax.numpy as jnp
from jax import lax
from jax.experimental import pallas as pl
from jax.experimental.pallas import tpu as pltpu
from jax.sharding import PartitionSpec as P

SEQ = 64
CAP = 2
MESH = pl.DeviceIdType.MESH
F32 = jnp.float32
BF16 = jnp.bfloat16


def take_kernel(_, x_ref, o_ref):
    o_ref[...] = x_ref[...]


def take(x, index):
    block = (1,) + x.shape[1:]
    return pl.pallas_call(
        take_kernel,
        grid_spec=pltpu.PrefetchScalarGridSpec(
            num_scalar_prefetch=1,
            grid=(index.shape[0],),
            in_specs=[pl.BlockSpec(block, lambda i, index_ref: (index_ref[i], 0, 0))],
            out_specs=pl.BlockSpec(block, lambda i, index_ref: (i, 0, 0)),
        ),
        out_shape=jax.ShapeDtypeStruct((index.shape[0],) + x.shape[1:], x.dtype),
    )(index, x)


def routing(index, resident_count, block_count):
    owner = index // (resident_count * block_count)
    local = index % resident_count
    positions = jnp.arange(index.shape[-1], dtype=jnp.int32)
    same = owner[..., :, None] == owner[..., None, :]
    earlier = positions[None, :] < positions[:, None]
    rank = jnp.sum(jnp.where(same & earlier, 1, 0), axis=-1).astype(jnp.int32)
    return owner, local, rank


def padded_path(tokens, weight, down, up, index):
    wide_count = lax.axis_size("wide")
    req_count = index.shape[0]
    owner, local, rank = routing(index, down.shape[0], lax.axis_size("blk"))
    slot_count = wide_count * CAP
    base = jnp.dot(
        tokens,
        lax.all_gather(weight, "blk", axis=0, tiled=True),
        preferred_element_type=F32,
    )
    positions = jnp.arange(req_count, dtype=jnp.int32)
    slot_of_req = owner * CAP + rank
    member = slot_of_req[:, None] == jnp.arange(slot_count, dtype=jnp.int32)[None, :]
    source_req = jnp.sum(jnp.where(member, positions[:, None], 0), axis=0)
    slot_local = jnp.sum(jnp.where(member, local[:, None], 0), axis=0)[:, None]
    outgoing = take(tokens.reshape(req_count, SEQ, tokens.shape[1]), source_req)
    arrived = lax.all_to_all(outgoing, "wide", split_axis=0, concat_axis=0, tiled=True)
    ids = lax.all_to_all(slot_local, "wide", split_axis=0, concat_axis=0, tiled=True)[:, 0]
    shrink = jnp.einsum(
        "sqd,srd->sqr", arrived, take(down, ids), preferred_element_type=F32
    ).astype(BF16)
    expand = jnp.einsum(
        "sqr,srk->sqk", shrink, take(up, ids), preferred_element_type=F32
    ).astype(BF16)
    returned = lax.all_to_all(expand, "wide", split_axis=0, concat_axis=0, tiled=True)
    delta = take(returned, slot_of_req).reshape(tokens.shape[0], up.shape[2])
    return (base + delta.astype(F32)).astype(BF16)


def fused_kernel(
    n, m,
    ids_ref, slot_ref, tokens_hbm, pack_hbm, weight_hbm, down_hbm, up_hbm,
    out_ref,
    tokens, weight, down, up, arrived, total, delta, returned,
    local_sem, rx_send, rx_recv, fwd_send, ret_send, ret_recv,
    own_send, chain_send, chain_recv, mate_send, mate_recv,
):
    w, p = lax.axis_index("wide"), lax.axis_index("blk")
    depth = weight_hbm.shape[0]
    half = depth // 2
    width, columns = tokens.shape[1], out_ref.shape[1]
    reqs = slot_ref.shape[0]
    core = lax.rem(w, 2)

    def partner(j):
        bits = [lax.rem(w // (1 << i), 2) for i in range((n - 1).bit_length())]
        return sum(
            ((1 - bit) if (j >> i) & 1 else bit) * (1 << i) for i, bit in enumerate(bits)
        )

    mate = partner(1)

    locals_ = [
        pltpu.make_async_copy(
            weight_hbm,
            weight.at[pl.ds(pl.multiple_of(p * depth, depth), depth)],
            local_sem.at[0],
        ),
        pltpu.make_async_copy(tokens_hbm, tokens, local_sem.at[1]),
        pltpu.make_async_copy(down_hbm, down, local_sem.at[2]),
        pltpu.make_async_copy(up_hbm, up, local_sem.at[3]),
        pltpu.make_async_copy(pack_hbm.at[w], arrived.at[w], local_sem.at[4]),
        pltpu.make_async_copy(pack_hbm.at[n], arrived.at[n + w], local_sem.at[5]),
    ]

    barrier = pltpu.get_barrier_semaphore()
    for j in range(1, n):
        pl.semaphore_signal(barrier, inc=1, device_id=(partner(j), p), device_id_type=MESH)
    for q in (lax.rem(p + 1, m), lax.rem(p + m - 1, m)):
        pl.semaphore_signal(barrier, inc=1, device_id=(w, q), device_id_type=MESH)
    for copy in locals_:
        copy.start()
    pl.semaphore_wait(barrier, n + 1)

    def remote(src, dst, send, recv, device):
        return pltpu.make_async_remote_copy(
            src_ref=src, dst_ref=dst, send_sem=send, recv_sem=recv,
            device_id=device, device_id_type=MESH,
        )

    def rows(k, side):
        return pl.ds(pl.multiple_of(k * depth + side * half, half), half)

    def own_copy(q, i):
        src = weight_hbm.at[pl.ds(pl.multiple_of(core * half, half), half)]
        return remote(src, weight.at[rows(p, core)], own_send.at[i], chain_recv.at[p], (w, q))

    def chain_copy(k, q):
        ref = weight.at[rows(k, core)]
        return remote(ref, ref, chain_send.at[k], chain_recv.at[k], (w, q))

    def mate_copy(k, side):
        ref = weight.at[rows(k, side)]
        return remote(ref, ref, mate_send.at[k], mate_recv.at[k], (mate, p))

    def slot_copy(j):
        q = partner(j)
        return remote(pack_hbm.at[q], arrived.at[w], rx_send.at[j], rx_recv.at[w], (q, p))

    def over_copy(j):
        return remote(
            pack_hbm.at[n], arrived.at[n + w], rx_send.at[n + j], rx_recv.at[n + w],
            (partner(j), p),
        )

    def forward_copy(j):
        ref = arrived.at[n + partner(j)]
        return remote(ref, ref, fwd_send.at[j], rx_recv.at[n + partner(j)], (mate, p))

    def wait_rows(slot):
        remote(
            arrived.at[slot], arrived.at[slot], rx_send.at[0], rx_recv.at[slot], (mate, p)
        ).wait_recv()

    def return_copy(j, over):
        q = partner(j)
        return remote(
            delta.at[over * n + q], returned.at[over * n + w],
            ret_send.at[over * n + j], ret_recv.at[over * n + w], (q, p),
        )

    even = [j for j in range(2, n) if j % 2 == 0]
    odd = [j for j in range(2, n) if j % 2 == 1]

    @pl.when(p + 1 < m)
    def _():
        own_copy(p + 1, 0).start()

    @pl.when(p > 0)
    def _():
        own_copy(p - 1, 1).start()

    for j in even:
        over_copy(j).start()
    over_copy(1).start()
    slot_copy(1).start()
    for j in even:
        slot_copy(j).start()

    tile = 256

    def add_base(start, length):
        at = pl.ds(pl.multiple_of(start, 128), length)

        @pl.loop(0, columns // tile)
        def _(t):
            c = pl.ds(pl.multiple_of(t * tile, tile), tile)
            total[:, c] += jnp.dot(tokens[:, at], weight[at, c], preferred_element_type=F32)

    step = min(2048, width)

    def adapter(slot, out):
        a = ids_ref[slot]

        def body(c, acc):
            at = pl.ds(pl.multiple_of(c * step, step), step)
            return acc + lax.dot_general(
                arrived[slot, :, at], down[a, :, at], (((1,), (1,)), ((), ())),
                preferred_element_type=F32,
            )

        shrink = lax.fori_loop(
            0, width // step, body, jnp.zeros((SEQ, down.shape[1]), F32)
        ).astype(BF16)
        out[slot] = jnp.dot(shrink, up[a], preferred_element_type=F32).astype(BF16)

    def serve(j, over):
        adapter(over * n + partner(j), delta)
        return_copy(j, over).start()

    def chain(d):
        for exists, k, more, q in (
            (p - d >= 0, p - d, p + 1 < m, p + 1),
            (p + d < m, p + d, p > 0, p - 1),
        ):

            @pl.when(exists)
            def _():
                chain_copy(k, lax.rem(p + 1, m)).wait_recv()
                mate_copy(k, core).start()

                @pl.when(more)
                def _():
                    chain_copy(k, q).start()

    def chain_compute(d):
        for exists, k in ((p - d >= 0, p - d), (p + d < m, p + d)):

            @pl.when(exists)
            def _():
                add_base(k * depth + core * half, half)
                mate_copy(k, 1 - core).wait_recv()
                add_base(k * depth + (1 - core) * half, half)

    total[...] = jnp.zeros_like(total)
    for i in (0, 1):
        locals_[i].wait()
    add_base(p * depth, half)
    add_base(p * depth + half, half)
    for i in (2, 3, 4, 5):
        locals_[i].wait()
    adapter(w, returned)
    adapter(n + w, returned)
    wait_rows(mate)
    serve(1, 0)
    wait_rows(n + mate)
    serve(1, 1)

    chain(1)
    for j in odd:
        slot_copy(j).start()
    chain_compute(1)
    for j in even:
        wait_rows(n + partner(j))
        forward_copy(j).start()
    for j in even:
        serve(j, 1)
    if m > 2:
        chain(2)
        chain_compute(2)
    for j in odd:
        wait_rows(n + partner(j))
        serve(j, 1)
    for j in even + odd:
        wait_rows(partner(j))
        serve(j, 0)

    @pl.loop(3, m)
    def _(d):
        chain(d)
        chain_compute(d)

    for over in (0, 1):
        for j in range(1, n):
            slot = over * n + partner(j)
            remote(
                delta.at[slot], returned.at[slot], ret_send.at[0], ret_recv.at[slot], (mate, p)
            ).wait_recv()

    @pl.loop(0, reqs)
    def _(r):
        at = pl.ds(pl.multiple_of(r * SEQ, SEQ), SEQ)
        out_ref[at] = (total[at] + returned[slot_ref[r]].astype(F32)).astype(out_ref.dtype)

    @pl.when(p + 1 < m)
    def _():
        own_copy(p + 1, 0).wait_send()

    @pl.when(p > 0)
    def _():
        own_copy(p - 1, 1).wait_send()

    @pl.loop(1, m)
    def _(d):
        for exists, k, more, q in (
            (p - d >= 0, p - d, p + 1 < m, p + 1),
            (p + d < m, p + d, p > 0, p - 1),
        ):

            @pl.when(exists)
            def _():
                mate_copy(k, core).wait_send()

                @pl.when(more)
                def _():
                    chain_copy(k, q).wait_send()

    for j in range(1, n):
        slot_copy(j).wait_send()
        return_copy(j, 0).wait_send()
        return_copy(j, 1).wait_send()
    over_copy(1).wait_send()
    for j in even:
        over_copy(j).wait_send()
        forward_copy(j).wait_send()


def fused_path(tokens, weight, down, up, pack, ids, slot_of_req):
    n, m = lax.axis_size("wide"), lax.axis_size("blk")
    rows, width = tokens.shape
    columns = weight.shape[1]
    any_spec = pl.BlockSpec(memory_space=pl.ANY)
    smem = pl.BlockSpec(memory_space=pltpu.SMEM)
    dma = pltpu.SemaphoreType.DMA
    return pl.pallas_call(
        functools.partial(fused_kernel, n, m),
        out_shape=jax.ShapeDtypeStruct((rows, columns), BF16),
        in_specs=[smem, smem] + [any_spec] * 5,
        out_specs=pl.BlockSpec(memory_space=pltpu.VMEM),
        scratch_shapes=[
            pltpu.VMEM((rows, width), BF16),
            pltpu.VMEM((width, columns), BF16),
            pltpu.VMEM(down.shape, BF16),
            pltpu.VMEM(up.shape, BF16),
            pltpu.VMEM((2 * n, SEQ, width), BF16),
            pltpu.VMEM((rows, columns), F32),
            pltpu.VMEM((2 * n, SEQ, columns), BF16),
            pltpu.VMEM((2 * n, SEQ, columns), BF16),
            dma((6,)), dma((2 * n,)), dma((2 * n,)), dma((n,)), dma((2 * n,)), dma((2 * n,)),
            dma((2,)), dma((m,)), dma((m,)), dma((m,)), dma((m,)),
        ],
        compiler_params=pltpu.CompilerParams(
            collective_id=0, has_side_effects=True, vmem_limit_bytes=60 * 2**20
        ),
    )(ids, slot_of_req, tokens, pack, weight, down, up)


def per_device(tokens, weight, down, up, index):
    n, m = lax.axis_size("wide"), lax.axis_size("blk")
    w, p = lax.axis_index("wide"), lax.axis_index("blk")
    req_count = index.shape[0]
    resident = down.shape[0]
    owner, local, rank = routing(index, resident, m)
    positions = jnp.arange(req_count, dtype=jnp.int32)
    first = (owner[:, None] == jnp.arange(n, dtype=jnp.int32)) & (rank == 0)[:, None]
    source = jnp.concatenate([
        jnp.sum(jnp.where(first, positions[:, None], 0), axis=0),
        jnp.max(jnp.where(rank == 1, positions, 0))[None],
    ]).astype(jnp.int32)
    pack = take(tokens.reshape(req_count, SEQ, tokens.shape[1]), source)

    everyone = lax.all_gather(index, ("wide", "blk"), axis=0).reshape(n, m, req_count)
    owners, locals_, ranks = routing(everyone, resident, m)
    fits = jnp.all(jnp.sum(ranks, axis=-1) <= 1)
    mine = (owners == w) & (jnp.arange(m, dtype=jnp.int32) == p)[None, :, None]
    ids = jnp.concatenate([
        jnp.sum(jnp.where(mine & (ranks == k), locals_, 0), axis=(1, 2)) for k in range(CAP)
    ]).astype(jnp.int32)
    return lax.cond(
        fits,
        lambda: fused_path(tokens, weight, down, up, pack, ids, owner + n * rank),
        lambda: padded_path(tokens, weight, down, up, index),
    )


def solution(mesh):
    return jax.shard_map(
        per_device,
        mesh=mesh,
        in_specs=(
            P(("wide", "blk"), None),
            P("blk", None),
            P(("wide", "blk"), None, None),
            P(("wide", "blk"), None, None),
            P(("wide", "blk")),
        ),
        out_specs=P(("wide", "blk"), None),
        check_vma=False,
    )
```

time: 321 us -> 240 us (0.75)
  waiting for transfers between devices: 214 us -> 0 us
  Pallas kernels: 0 us -> 177 us
  blocking collectives: 0 us -> 40.6 us
  matrix products: 30.2 us -> 0 us
  local copies, waits for them, and re-layouts: 26.9 us -> 2.24 us
  starting transfers between devices: 17.9 us -> 0 us
  other arithmetic: 18.2 us -> 5.84 us
    all_to_all x3 -> x0, waiting for transfers between devices: 191 us -> none  [the longest x1 168 us: per_device(): lax.all_to_all(outgoing, 'wide', split_axis=0, concat_axis=0, tiled=True)]
    pallas_call x0 -> x2, Pallas kernels: none -> 177 us  [the longest x1 165 us: fused_path(): pl.pallas_call(functools.partial(fused_kernel, n, m), out_shape=jax.Shape...]
    unnamed x0 -> x1, blocking collectives: none -> 40.6 us
    dot_general x2 -> x0, matrix products: 30.2 us -> none  [the longest x1 15.6 us: per_device(): jnp.dot(tokens, lax.all_gather(base_key_matrix, 'blk', axis=0, tiled=True...]
    gather x6 -> x0, local copies, waits for them, and re-layouts: 25.9 us -> none  [the longest x1 12.4 us: per_device(): outgoing = jnp.take(requests, source_req, axis=0)]
    all_gather x1 -> x0, waiting for transfers between devices: 22.2 us -> none  [per_device(): lax.all_gather(base_key_matrix, 'blk', axis=0, tiled=True)]
    all_to_all x3 -> x0, starting transfers between devices: 17.9 us -> none  [the longest x1 7.06 us: per_device(): lax.all_to_all(expand, 'wide', split_axis=0, concat_axis=0, tiled=True)]
    select_n x9 -> x2, other arithmetic: 17.2 us -> 0.69 us  [routing(): owner = index // (resident_count * block_count)]
  transfers between devices with their start and end apart: 4 -> 0, of which waited for: 3 -> 0; matrix products, arithmetic and copies ran while one was open for 19% -> 0% of each run, Pallas kernels for 0% -> 0%
where the time goes in v1:
time: 240 us
  Pallas kernels  177 us (74%)
  blocking collectives  40.6 us (17%)
  between operations  14.1 us (6%)
  other arithmetic  5.84 us (2%)
    pallas_call x1, Pallas kernels, fused_path(): pl.pallas_call(functools.partial(fused_kernel, n, m), out_shape=jax.Shape...  165 us
    unnamed x1, blocking collectives  40.6 us
    pallas_call x1, Pallas kernels, take(): pl.pallas_call(take_kernel, grid_spec=pltpu.PrefetchScalarGridSpec(num_sc...  11.6 us

profile of v1, /device:TPU:1, one launch (start us, length us, event | category | flops | bytes accessed | tf_op | source)
XLA Modules:
  0.0 239.7 jit_solution(5612830773454348078)
XLA Ops:
  6.5 0.8 dynamic-update-slice
  7.4 40.6 %all-reduce = s32[256]{0:T(256)S(1)} all-reduce(s32[256]{0:T(256)S(1)} %dynamic-update-slice), channel_id=2, replica_groups=mesh['wide'=8,'blk'=4] {'wide','blk'}, use_global_device_ids=true, to_apply=%add | all-reduce | flops 256 | bytes 2048
  47.9 0.1 reshape.107
  48.1 1.3 select_reduce_fusion.3
  49.4 0.6 compare_reduce_fusion
  50.7 0.7 and_select_fusion.2
  51.3 0.2 select_reduce_fusion.8
  51.5 0.1 reshape.110
  51.6 0.1 and.101
  51.7 0.2 select_reduce_fusion.6
  51.9 0.1 reduce_sum.102
  52.0 0.1 reduce_sum.103
  52.1 0.1 reduce_sum.99
  52.2 0.1 reduce_sum.100
  52.3 0.1 pad_add_fusion
  52.4 0.6 fusion.9
  53.0 0.1 select_reduce_fusion.7
  53.1 1.3 pad_add_fusion.1._
  54.4 0.0 copy-start.1
  54.4 0.0 copy-start.3
  54.4 11.6 %shard_map.57 = bf16[9,64,8192]{2,1,0:T(8,128)(2,1)} custom-call(s32[9]{0:T(128)} %pad_add_fusion.1._, bf16[8,64,8192]{2,1,0:T(8,128)(2,1)} %bitcast.14), custom_call_target="tpu_custom_call" | custom-call | tf_op jit(solution)/shard_map/pallas_call | solution.py:23
  66.0 0.0 copy-done.1
  66.0 0.0 copy-done.3
  66.0 165.8 %conditional.1 = (bf16[512,1024]{1,0:T(8,128)(2,1)S(1)}) conditional(s32[]{:T(128)} %convert_element_type.18, (bf16[2048,1024]{1,0:T(8,128)(2,1)}, bf16[512,8192]{1,0:T(8,128)(2,1)}, s32[8]{0:T(128)S(1)}, bf16[8,64,8192]{2,1,0:T(8,128)(2,1)}, bf16[8,64,1024]{2,1,0:T(8,128)(2,1)S(1)}) %tuple.26, (s32[8]{0:T(128)S(1)}, s32[8]{0:T(128)S(1)}, ...), branch_computations={%region_10.14_spmd, %region_14.15_spmd} | conditional | flops 9800582144 | bytes 190850240 | solution.py:373
  66.0 0.5 multiply_add_fusion.slot_ref
  66.6 165.1 %branch_1_fun.1 = bf16[512,1024]{1,0:T(8,128)(2,1)S(1)} custom-call(s32[16]{0:T(128)S(1)} %get-tuple-element.39.ids_ref, s32[8]{0:T(128)} %multiply_add_fusion.slot_ref, bf16[512,8192]{1,0:T(8,128)(2,1)} %get-tuple-element.42.tokens_hbm, bf16[9,64,8192]{2,1,0:T(8,128)(2,1)} %get-tuple-element.43.pack_hbm, bf16[2048,1024]{1,0:T(8,128)(2,1)} %get-tuple-element.44.weight_hbm, ...), custom_call_target="tpu_custom_call" | custom-call | tf_op jit(solution)/shard_map/cond/branch_1_fun/pallas_call | solution.py:329
  231.9 1.0 copy.16
  (7 shorter events, 0.1 us)
Async XLA Ops:
  54.4 11.6 %copy-start.1 = (bf16[8,64,1024]{2,1,0:T(8,128)(2,1)S(1)}, bf16[8,64,1024]{2,1,0:T(8,128)(2,1)}, u32[]{:S(2)}) copy-start(bf16[8,64,1024]{2,1,0:T(8,128)(2,1)} %param.10) | copy-start | bytes 3145732
  54.4 11.6 %copy-start.3 = (s32[8]{0:T(128)S(1)}, s32[8]{0:T(128)}, u32[]{:S(2)}) copy-start(s32[8]{0:T(128)} %param.11) | copy-start | bytes 100

commit v2 on v1

--- a/solution.py
+++ b/solution.py
@@ -9,6 +9,8 @@
 
 SEQ = 64
 CAP = 2
+PACK_PARTS = 4
+PIECES = 2
 MESH = pl.DeviceIdType.MESH
 F32 = jnp.float32
 BF16 = jnp.bfloat16
@@ -29,6 +31,50 @@
             out_specs=pl.BlockSpec(block, lambda i, index_ref: (i, 0, 0)),
         ),
         out_shape=jax.ShapeDtypeStruct((index.shape[0],) + x.shape[1:], x.dtype),
+    )(index, x)
+
+
+def pack_kernel(index_ref, x_ref, o_ref, held, in_sems, out_sems):
+    parts, count = in_sems.shape[0], o_ref.shape[0]
+    part = x_ref.shape[2] // parts
+    at = [pl.ds(c * part, part) for c in range(parts)]
+    arrivals = [
+        pltpu.make_async_copy(x_ref.at[:, :, at[c]], held.at[:, :, at[c]], in_sems.at[c])
+        for c in range(parts)
+    ]
+    for copy in arrivals:
+        copy.start()
+    copies = []
+    for c in range(parts):
+        arrivals[c].wait()
+        for i in range(count):
+            copy = pltpu.make_async_copy(
+                held.at[index_ref[i], :, at[c]], o_ref.at[i, :, at[c]], out_sems.at[c, i]
+            )
+            copy.start()
+            copies.append(copy)
+    for copy in copies:
+        copy.wait()
+
+
+def pack_rows(x, index):
+    count = index.shape[0]
+    size = count * x.shape[1] * x.shape[2]
+    return pl.pallas_call(
+        pack_kernel,
+        in_specs=[
+            pl.BlockSpec(memory_space=pltpu.SMEM),
+            pl.BlockSpec(memory_space=pl.ANY),
+        ],
+        out_specs=pl.BlockSpec(memory_space=pl.ANY),
+        out_shape=jax.ShapeDtypeStruct((count,) + x.shape[1:], x.dtype),
+        scratch_shapes=[
+            pltpu.VMEM(x.shape, x.dtype),
+            pltpu.SemaphoreType.DMA((PACK_PARTS,)),
+            pltpu.SemaphoreType.DMA((PACK_PARTS, count)),
+        ],
+        compiler_params=pltpu.CompilerParams(vmem_limit_bytes=16 * 2**20),
+        cost_estimate=pl.CostEstimate(flops=0, bytes_accessed=4 * size, transcendentals=0),
     )(index, x)
 
 
@@ -77,11 +123,12 @@
     out_ref,
     tokens, weight, down, up, arrived, total, delta, returned,
     local_sem, rx_send, rx_recv, fwd_send, ret_send, ret_recv,
-    own_send, chain_send, chain_recv, mate_send, mate_recv,
+    own_send, chain_send, chain_recv, mate_send, mate_recv, cross_send, cross_recv,
 ):
     w, p = lax.axis_index("wide"), lax.axis_index("blk")
     depth = weight_hbm.shape[0]
     half = depth // 2
+    piece = half // PIECES
     width, columns = tokens.shape[1], out_ref.shape[1]
     reqs = slot_ref.shape[0]
     core = lax.rem(w, 2)
@@ -122,20 +169,23 @@
             device_id=device, device_id_type=MESH,
         )
 
-    def rows(k, side):
-        return pl.ds(pl.multiple_of(k * depth + side * half, half), half)
-
-    def own_copy(q, i):
-        src = weight_hbm.at[pl.ds(pl.multiple_of(core * half, half), half)]
-        return remote(src, weight.at[rows(p, core)], own_send.at[i], chain_recv.at[p], (w, q))
-
-    def chain_copy(k, q):
-        ref = weight.at[rows(k, core)]
-        return remote(ref, ref, chain_send.at[k], chain_recv.at[k], (w, q))
-
-    def mate_copy(k, side):
-        ref = weight.at[rows(k, side)]
-        return remote(ref, ref, mate_send.at[k], mate_recv.at[k], (mate, p))
+    def rows(k, side, i):
+        return pl.ds(pl.multiple_of(k * depth + side * half + i * piece, piece), piece)
+
+    def own_copy(q, left, i):
+        src = weight_hbm.at[pl.ds(pl.multiple_of(core * half + i * piece, piece), piece)]
+        return remote(
+            src, weight.at[rows(p, core, i)], own_send.at[left, i],
+            chain_recv.at[p, i], (w, q),
+        )
+
+    def chain_copy(k, q, i):
+        ref = weight.at[rows(k, core, i)]
+        return remote(ref, ref, chain_send.at[k, i], chain_recv.at[k, i], (w, q))
+
+    def mate_copy(k, side, i):
+        ref = weight.at[rows(k, side, i)]
+        return remote(ref, ref, mate_send.at[k, i], mate_recv.at[k, i], (mate, p))
 
     def slot_copy(j):
         q = partner(j)
@@ -146,6 +196,16 @@
             pack_hbm.at[n], arrived.at[n + w], rx_send.at[n + j], rx_recv.at[n + w],
             (partner(j), p),
         )
+
+    def cross_copy(i):
+        near, far = (2, 4) if i == 0 else (4, 2)
+        slot = n + partner(near)
+        ref = arrived.at[slot, :, pl.ds(i * (width // 2), width // 2)]
+        return remote(ref, ref, cross_send.at[i], cross_recv.at[i], (partner(far), p))
+
+    def wait_cross(i):
+        ref = arrived.at[n + partner(6), :, pl.ds(i * (width // 2), width // 2)]
+        remote(ref, ref, cross_send.at[i], cross_recv.at[i], (mate, p)).wait_recv()
 
     def forward_copy(j):
         ref = arrived.at[n + partner(j)]
@@ -168,13 +228,15 @@
 
     @pl.when(p + 1 < m)
     def _():
-        own_copy(p + 1, 0).start()
+        for i in range(PIECES):
+            own_copy(p + 1, 0, i).start()
 
     @pl.when(p > 0)
     def _():
-        own_copy(p - 1, 1).start()
-
-    for j in even:
+        for i in range(PIECES):
+            own_copy(p - 1, 1, i).start()
+
+    for j in (2, 4):
         over_copy(j).start()
     over_copy(1).start()
     slot_copy(1).start()
@@ -212,28 +274,34 @@
         adapter(over * n + partner(j), delta)
         return_copy(j, over).start()
 
-    def chain(d):
-        for exists, k, more, q in (
+    def ways(d):
+        return (
             (p - d >= 0, p - d, p + 1 < m, p + 1),
             (p + d < m, p + d, p > 0, p - 1),
-        ):
-
-            @pl.when(exists)
-            def _():
-                chain_copy(k, lax.rem(p + 1, m)).wait_recv()
-                mate_copy(k, core).start()
-
-                @pl.when(more)
+        )
+
+    def chain(d):
+        for i in range(PIECES):
+            for exists, k, more, q in ways(d):
+
+                @pl.when(exists)
                 def _():
-                    chain_copy(k, q).start()
+                    chain_copy(k, lax.rem(p + 1, m), i).wait_recv()
+
+                    @pl.when(more)
+                    def _():
+                        chain_copy(k, q, i).start()
+
+                    mate_copy(k, core, i).start()
 
     def chain_compute(d):
-        for exists, k in ((p - d >= 0, p - d), (p + d < m, p + d)):
+        for exists, k, _, _ in ways(d):
 
             @pl.when(exists)
             def _():
                 add_base(k * depth + core * half, half)
-                mate_copy(k, 1 - core).wait_recv()
+                for i in range(PIECES):
+                    mate_copy(k, 1 - core, i).wait_recv()
                 add_base(k * depth + (1 - core) * half, half)
 
     total[...] = jnp.zeros_like(total)
@@ -254,18 +322,26 @@
     for j in odd:
         slot_copy(j).start()
     chain_compute(1)
-    for j in even:
+    for i, j in enumerate((2, 4)):
         wait_rows(n + partner(j))
+        cross_copy(i).start()
         forward_copy(j).start()
-    for j in even:
+    for j in (2, 4):
         serve(j, 1)
     if m > 2:
         chain(2)
         chain_compute(2)
+    for i in (0, 1):
+        wait_cross(i)
+    forward_copy(6).start()
+    serve(6, 1)
+    for j in even:
+        wait_rows(partner(j))
+        serve(j, 0)
     for j in odd:
         wait_rows(n + partner(j))
         serve(j, 1)
-    for j in even + odd:
+    for j in odd:
         wait_rows(partner(j))
         serve(j, 0)
 
@@ -288,34 +364,37 @@
 
     @pl.when(p + 1 < m)
     def _():
-        own_copy(p + 1, 0).wait_send()
+        for i in range(PIECES):
+            own_copy(p + 1, 0, i).wait_send()
 
     @pl.when(p > 0)
     def _():
-        own_copy(p - 1, 1).wait_send()
+        for i in range(PIECES):
+            own_copy(p - 1, 1, i).wait_send()
 
     @pl.loop(1, m)
     def _(d):
-        for exists, k, more, q in (
-            (p - d >= 0, p - d, p + 1 < m, p + 1),
-            (p + d < m, p + d, p > 0, p - 1),
-        ):
+        for exists, k, more, q in ways(d):
 
             @pl.when(exists)
             def _():
-                mate_copy(k, core).wait_send()
+                for i in range(PIECES):
+                    mate_copy(k, core, i).wait_send()
 
                 @pl.when(more)
                 def _():
-                    chain_copy(k, q).wait_send()
+                    for i in range(PIECES):
+                        chain_copy(k, q, i).wait_send()
 
     for j in range(1, n):
         slot_copy(j).wait_send()
         return_copy(j, 0).wait_send()
         return_copy(j, 1).wait_send()
     over_copy(1).wait_send()
+    for i, j in enumerate((2, 4)):
+        over_copy(j).wait_send()
+        cross_copy(i).wait_send()
     for j in even:
-        over_copy(j).wait_send()
         forward_copy(j).wait_send()
 
 
@@ -341,7 +420,8 @@
             pltpu.VMEM((2 * n, SEQ, columns), BF16),
             pltpu.VMEM((2 * n, SEQ, columns), BF16),
             dma((6,)), dma((2 * n,)), dma((2 * n,)), dma((n,)), dma((2 * n,)), dma((2 * n,)),
-            dma((2,)), dma((m,)), dma((m,)), dma((m,)), dma((m,)),
+            dma((2, PIECES)), dma((m, PIECES)), dma((m, PIECES)), dma((m, PIECES)), dma((m, PIECES)),
+            dma((2,)), dma((2,)),
         ],
         compiler_params=pltpu.CompilerParams(
             collective_id=0, has_side_effects=True, vmem_limit_bytes=60 * 2**20
@@ -361,9 +441,12 @@
         jnp.sum(jnp.where(first, positions[:, None], 0), axis=0),
         jnp.max(jnp.where(rank == 1, positions, 0))[None],
     ]).astype(jnp.int32)
-    pack = take(tokens.reshape(req_count, SEQ, tokens.shape[1]), source)
-
-    everyone = lax.all_gather(index, ("wide", "blk"), axis=0).reshape(n, m, req_count)
+    pack = pack_rows(tokens.reshape(req_count, SEQ, tokens.shape[1]), source)
+
+    everyone = lax.all_to_all(
+        jnp.broadcast_to(index, (n * m, req_count)),
+        ("wide", "blk"), split_axis=0, concat_axis=0, tiled=True,
+    ).reshape(n, m, req_count)
     owners, locals_, ranks = routing(everyone, resident, m)
     fits = jnp.all(jnp.sum(ranks, axis=-1) <= 1)
     mine = (owners == w) & (jnp.arange(m, dtype=jnp.int32) == p)[None, :, None]

time: 240 us -> 192 us (0.80)
  blocking collectives: 40.6 us -> 0 us
  Pallas kernels: 177 us -> 163 us
  starting transfers between devices: 0 us -> 7.1 us
    unnamed x1 -> x0, blocking collectives: 40.6 us -> none
    pallas_call x1, Pallas kernels: 165 us -> 155 us  [fused_path(): pl.pallas_call(functools.partial(fused_kernel, n, m), out_shape=jax.Shape...]
    all_to_all x0 -> x1, starting transfers between devices: none -> 7.1 us  [per_device(): lax.all_to_all(jnp.broadcast_to(index, (n * m, req_count)), ('wide', 'blk...]
    pallas_call x1, Pallas kernels: 11.6 us -> 7.91 us  [pack_rows(): pl.pallas_call(pack_kernel, in_specs=[pl.BlockSpec(memory_space=pltpu.SME...]
  transfers between devices with their start and end apart: 0 -> 1, of which waited for: 0 -> 0; matrix products, arithmetic and copies ran while one was open for 0% -> 1% of each run, Pallas kernels for 0% -> 4%
where the time goes in v2:
time: 192 us
  Pallas kernels  163 us (85%)
  between operations  14.1 us (7%)
  starting transfers between devices  7.1 us (4%)
  other arithmetic  5.41 us (3%)
  local copies, waits for them, and re-layouts  2.5 us (1%)
    pallas_call x1, Pallas kernels, fused_path(): pl.pallas_call(functools.partial(fused_kernel, n, m), out_shape=jax.Shape...  155 us
    pallas_call x1, Pallas kernels, pack_rows(): pl.pallas_call(pack_kernel, in_specs=[pl.BlockSpec(memory_space=pltpu.SME...  7.91 us
    all_to_all x1, starting transfers between devices, per_device(): lax.all_to_all(jnp.broadcast_to(index, (n * m, req_count)), ('wide', 'blk...  7.1 us
  transfers between devices with their start and end apart: 1, of which 0 were waited for; matrix products, arithmetic and copies ran while one was open for 1% of the time, Pallas kernels for 4%

profile of v2, /device:TPU:1, one launch (start us, length us, event | category | flops | bytes accessed | tf_op | source)
XLA Modules:
  0.0 192.1 jit_solution(10865263653658040047)
XLA Ops:
  6.5 1.3 broadcast_in_dim.82
  7.8 7.1 %all-to-all-start.3 = ((s32[32,1,8]{2,1,0:T(1,128)}), s32[32,1,8]{2,1,0:T(1,128)S(1)}, u32[]{:S(2)}, u32[]{:S(2)}) async-start(s32[32,1,8]{2,1,0:T(1,128)} %broadcast_in_dim.82), calls=%async_computation.3 | async-start | bytes 32768 | tf_op jit(solution)/shard_map/all_to_all | solution.py:446
  14.9 0.7 and_select_fusion.2
  15.6 0.2 select_reduce_fusion.8
  15.8 0.7 fusion.9
  16.5 0.1 select_reduce_fusion.7
  16.6 0.8 pad_add_fusion.1.index_ref
  17.4 0.1 and.101
  17.4 0.0 copy-start.1
  17.4 0.0 copy-start.3
  17.5 7.9 %shard_map.57 = bf16[9,64,8192]{2,1,0:T(8,128)(2,1)} custom-call(s32[9]{0:T(128)S(1)} %pad_add_fusion.1.index_ref, bf16[8,64,8192]{2,1,0:T(8,128)(2,1)} %bitcast.16), custom_call_target="tpu_custom_call" | custom-call | bytes 18874368 | tf_op jit(solution)/shard_map/pallas_call | solution.py:63
  25.4 0.0 all-to-all-done.3
  25.4 1.3 select_reduce_fusion.3
  26.7 0.6 compare_reduce_fusion
  28.0 0.2 select_reduce_fusion.6
  28.2 0.1 reduce_sum.102
  28.3 0.1 reduce_sum.99
  28.4 0.1 reduce_sum.103
  28.5 0.1 reduce_sum.100
  28.6 0.1 pad_add_fusion
  28.7 0.0 copy-done.1
  28.7 0.0 copy-done.3
  28.7 155.6 %conditional.1 = (bf16[512,1024]{1,0:T(8,128)(2,1)S(1)}) conditional(s32[]{:T(128)} %convert_element_type.18, (bf16[2048,1024]{1,0:T(8,128)(2,1)}, bf16[512,8192]{1,0:T(8,128)(2,1)}, s32[8]{0:T(128)S(1)}, bf16[8,64,8192]{2,1,0:T(8,128)(2,1)}, bf16[8,64,1024]{2,1,0:T(8,128)(2,1)S(1)}) %tuple.26, (s32[8]{0:T(128)S(1)}, s32[8]{0:T(128)S(1)}, ...), branch_computations={%region_10.14_spmd, %region_14.15_spmd} | conditional | flops 9800582144 | bytes 190850240 | solution.py:456
  28.7 0.5 multiply_add_fusion.slot_ref
  29.2 154.8 %branch_1_fun.1 = bf16[512,1024]{1,0:T(8,128)(2,1)S(1)} custom-call(s32[16]{0:T(128)S(1)} %get-tuple-element.39.ids_ref, s32[8]{0:T(128)} %multiply_add_fusion.slot_ref, bf16[512,8192]{1,0:T(8,128)(2,1)} %get-tuple-element.42.tokens_hbm, bf16[9,64,8192]{2,1,0:T(8,128)(2,1)} %get-tuple-element.43.pack_hbm, bf16[2048,1024]{1,0:T(8,128)(2,1)} %get-tuple-element.44.weight_hbm, ...), custom_call_target="tpu_custom_call" | custom-call | tf_op jit(solution)/shard_map/cond/branch_1_fun/pallas_call | solution.py:408
  184.3 1.0 copy.24
  (6 shorter events, 0.1 us)
Async XLA Ops:
  7.8 17.6 %all-to-all-start.3 = ((s32[32,1,8]{2,1,0:T(1,128)}), s32[32,1,8]{2,1,0:T(1,128)S(1)}, u32[]{:S(2)}, u32[]{:S(2)}) async-start(s32[32,1,8]{2,1,0:T(1,128)} %broadcast_in_dim.82), calls=%async_computation.3 | async-start | bytes 32768 | tf_op jit(solution)/shard_map/all_to_all | solution.py:446
  17.4 11.2 %copy-start.1 = (bf16[8,64,1024]{2,1,0:T(8,128)(2,1)S(1)}, bf16[8,64,1024]{2,1,0:T(8,128)(2,1)}, u32[]{:S(2)}) copy-start(bf16[8,64,1024]{2,1,0:T(8,128)(2,1)} %param.10) | copy-start | bytes 3145732
  17.4 11.2 %copy-start.3 = (s32[8]{0:T(128)S(1)}, s32[8]{0:T(128)}, u32[]{:S(2)}) copy-start(s32[8]{0:T(128)} %param.11) | copy-start | bytes 100
